TPU v7x, 32 devices: a whole 2x2x4 slice. The times are simulated.
32 devices in a mesh: region: 4 (over z), rows: 8 (over y, x, core).
Axes of the slice: x: 2, y: 2, z: 4, core: 2. Of those that a mesh axis runs over, the one named last changes fastest.
Arguments:
- ensemble_state: float32 [65536, 256], P(('region', 'rows')), may hold values from -16 to 16
- obs_values: float32 [4, 1024], replicated, may hold values from -16 to 16
- obs_error: float32 [4, 1024], replicated, may hold values from 0.1 to 2
- batch_owner: int32 [4], replicated, may hold values from 0 to 3
- readers: int32 [4, 3], replicated, may hold values from 0 to 3
- obs_order: int32 [4, 1024], replicated, may hold values from 0 to 1023, each once within a row
- obs_rows: int32 [4, 1024], replicated, may hold values from 0 to 2047
- loc_taper: float32 [4, 4, 1024], replicated, may hold values from 0.02 to 0.3
Outputs:
- analysis: float32 [65536, 256], P(('region', 'rows'))
Inputs may be any that keep to these rules, and one draw needn't show every extreme that they name: Each row of obs_order holds every observation number once. `readers`: regions that read a batch besides its owner region; repeats allowed.
All inputs are finite; a program needn't handle non-finite values.
Results may differ from a plain program's by a relative error of at most 0.0024.
Values may be sent and summed in bfloat16 or wider, within the bound.
A program may use at most 64 MiB of HBM per device.

v0:
```python
import jax
import jax.numpy as jnp
from jax import lax
from jax.sharding import PartitionSpec as P


def broadcast(value, axis, source):
    kept = jnp.where(lax.axis_index(axis) == source, value, 0).astype(value.dtype)
    return lax.psum(kept, axis)


def adjust(prior_ens, values, errors):
    members = prior_ens.shape[1]
    prior_mean = jnp.mean(prior_ens, axis=1, keepdims=True)
    anomalies = prior_ens - prior_mean
    variance = jnp.sum(anomalies * anomalies, axis=1, keepdims=True) / (members - 1) + 1e-05
    errors = errors[:, None]
    values = values[:, None]
    post_var = variance * errors / (variance + errors)
    mean_shift = post_var * (prior_mean / variance + values / errors) - prior_mean
    shrink = jnp.sqrt(errors / (variance + errors))
    obs_incr = (mean_shift + (shrink - 1.0) * anomalies).astype(jnp.bfloat16)
    scaled = (anomalies / ((members - 1) * variance)).astype(jnp.bfloat16)
    return (scaled, obs_incr)


def update_block(block_x, scaled, obs_incr, weights):
    centre = jnp.mean(block_x, axis=1, keepdims=True)
    state_anom = (block_x - centre).astype(jnp.bfloat16)
    linked = lax.dot_general(
        state_anom, scaled, (((1,), (1,)), ((), ())), preferred_element_type=jnp.float32
    )
    coupling = (linked * weights[None, :]).astype(jnp.bfloat16)
    return block_x + jnp.dot(coupling, obs_incr, preferred_element_type=jnp.float32)


def update_state(state_x, scaled, obs_incr, weights, reading):
    rows_total, members = state_x.shape
    block_rows = min(512, rows_total)

    def apply_all(current):
        split_blocks = current.reshape(rows_total // block_rows, block_rows, members)
        updated = lax.map(
            lambda single: update_block(single, scaled, obs_incr, weights), split_blocks
        )
        return updated.reshape(rows_total, members)

    return lax.cond(reading, apply_all, lambda current: current, state_x)


def local(
    ensemble_state, obs_values, obs_error, batch_owner, readers, obs_order, obs_rows, loc_taper
):
    group_size = lax.axis_size("rows")
    region_idx = lax.axis_index("region")
    column_idx = lax.axis_index("rows")
    batches, obs_count = obs_order.shape
    slot_count = obs_count // group_size
    members = ensemble_state.shape[1]
    current = ensemble_state
    for batch_idx in range(batches):
        pieces = current[
            lax.dynamic_slice_in_dim(obs_rows[batch_idx], column_idx * slot_count, slot_count)
        ]
        placed = lax.dynamic_slice_in_dim(obs_order[batch_idx], column_idx * slot_count, slot_count)
        padded = jnp.zeros((obs_count, members), jnp.float32).at[placed].set(pieces)
        prior_ens = lax.psum(padded, "rows")
        scaled, obs_incr = adjust(prior_ens, obs_values[batch_idx], obs_error[batch_idx])
        scaled, obs_incr = (
            broadcast(scaled, "region", batch_owner[batch_idx]),
            broadcast(obs_incr, "region", batch_owner[batch_idx]),
        )
        scaled, obs_incr = (scaled, obs_incr)
        current = update_state(
            current,
            scaled,
            obs_incr,
            lax.dynamic_index_in_dim(loc_taper[batch_idx], region_idx, 0, keepdims=False),
            jnp.logical_or(
                batch_owner[batch_idx] == region_idx, jnp.any(readers[batch_idx] == region_idx)
            ),
        )
    return current


def solution(mesh):
    placed = (P(("region", "rows"), None), P(), P(), P(), P(), P(), P(), P())
    return jax.shard_map(
        local, mesh=mesh, in_specs=placed, out_specs=P(("region", "rows"), None), check_vma=False
    )
```

profile of v0, /device:TPU:0, one launch (start us, length us, event | category | flops | bytes accessed | tf_op | source)
XLA Modules:
  0.0 533.8 jit_solution(5910269300166853925)
XLA Ops:
  6.5 1.6 copy.65
  8.3 2.4 scatter_custom_fusion
  10.7 0.0 all-reduce.27.cloned.1.call-start
  10.7 0.7 fusion.100
  12.1 58.0 %all-reduce.13.cloned.1.call-done = f32[1024,256]{1,0:T(8,128)} async-done(((f32[1024,256]{1,0:T(8,128)}), f32[1024,256]{1,0:T(8,128)}) %all-reduce.13.cloned.1.call-update) | async-done | bytes 1048592 | tf_op jit(solution)/shard_map/psum | solution.py:67
  70.1 1.5 reduce_sum.108
  71.7 1.6 multiply_reduce_fusion.3
  73.3 1.7 fusion.56
  75.7 0.7 compare_reduce_fusion
  77.1 49.4 %all-reduce.27.cloned.1.call-done = (bf16[1024,256]{1,0:T(8,128)(2,1)}, bf16[1024,256]{1,0:T(8,128)(2,1)}) async-done(((bf16[1024,256]{1,0:T(8,128)(2,1)}, bf16[1024,256]{1,0:T(8,128)(2,1)}), (bf16[1024,256]{1,0:T(8,128)(2,1)}, bf16[1024,256]{1,0:T(8,128)(2,1)})) %all-reduce.27.cloned.1.call-update) | async-done | bytes 1048592 | tf_op jit(solution)/shard_map/psum | solution.py:9
  126.5 13.7 %conditional.4 = (f32[2048,256]{1,0:T(8,128)S(1)}) conditional(s32[]{:T(128)} %convert_element_type.72, f32[2048,256]{1,0:T(8,128)S(1)} %copy.65, (f32[2048,256]{1,0:T(8,128)S(1)}, bf16[1024,256]{1,0:T(8,128)(2,1)}, f32[4,4,1024]{2,1,0:T(4,128)S(1)}, bf16[1024,256]{1,0:T(8,128)(2,1)}, s32[]{:T(128)}) %tuple.168), branch_computations={%region_10.11_spmd, %region_11.0_spmd.clone} | conditional | flops 538443776 | bytes 7394469 | solution.py:48
  126.5 12.1 %while.42 = (s32[]{:T(128)}, f32[4,512,256]{2,1,0:T(8,128)}, f32[4,512,256]{2,1,0:T(8,128)S(1)}, bf16[1024,256]{1,0:T(8,128)(2,1)}, f32[1024]{0:T(1024)S(1)}, /*index=5*/bf16[1024,256]{1,0:T(8,128)(2,1)}, s32[]{:T(128)}) while((s32[]{:T(128)}, f32[4,512,256]{2,1,0:T(8,128)}, f32[4,512,256]{2,1,0:T(8,128)S(1)}, ...), condition=%wide.region_14.14_spmd, body=%wide.region_12.13_spmd.sunk | while | flops 538443776 | bytes 3159129 | solution.py:43
  126.5 0.2 dynamic-slice_reduce_fusion.11
  126.7 2.9 fusion.140
  129.5 0.1 dynamic-slice_reduce_fusion.11
  129.7 2.9 fusion.140
  132.5 0.1 dynamic-slice_reduce_fusion.11
  132.7 2.9 fusion.140
  135.5 0.1 dynamic-slice_reduce_fusion.11
  135.7 2.9 fusion.140
  138.6 1.6 copy.43
  140.2 2.4 scatter_custom_fusion.1
  142.6 0.0 all-reduce.25.cloned.1.call-start
  143.3 55.4 %all-reduce.15.cloned.1.call-done = f32[1024,256]{1,0:T(8,128)} async-done(((f32[1024,256]{1,0:T(8,128)}), f32[1024,256]{1,0:T(8,128)}) %all-reduce.15.cloned.1.call-update) | async-done | bytes 1048592 | tf_op jit(solution)/shard_map/psum | solution.py:67
  198.7 1.5 reduce_sum.110
  200.2 1.6 multiply_reduce_fusion.2
  201.8 1.7 fusion.57
  205.0 50.0 %all-reduce.25.cloned.1.call-done = (bf16[1024,256]{1,0:T(8,128)(2,1)}, bf16[1024,256]{1,0:T(8,128)(2,1)}) async-done(((bf16[1024,256]{1,0:T(8,128)(2,1)}, bf16[1024,256]{1,0:T(8,128)(2,1)}), (bf16[1024,256]{1,0:T(8,128)(2,1)}, bf16[1024,256]{1,0:T(8,128)(2,1)})) %all-reduce.25.cloned.1.call-update) | async-done | bytes 1048592 | tf_op jit(solution)/shard_map/psum | solution.py:9
  255.0 13.7 %conditional.5 = (f32[2048,256]{1,0:T(8,128)S(1)}) conditional(s32[]{:T(128)} %convert_element_type.71, f32[2048,256]{1,0:T(8,128)S(1)} %get-tuple-element.607, (f32[2048,256]{1,0:T(8,128)S(1)}, bf16[1024,256]{1,0:T(8,128)(2,1)}, f32[4,4,1024]{2,1,0:T(4,128)S(1)}, bf16[1024,256]{1,0:T(8,128)(2,1)}, s32[]{:T(128)}) %tuple.169), branch_computations={%region_21.22_spmd, %region_22.26_spmd.clone} | conditional | flops 538443776 | bytes 7394469 | solution.py:48
  255.0 12.1 %while.43 = (s32[]{:T(128)}, f32[4,512,256]{2,1,0:T(8,128)}, f32[4,512,256]{2,1,0:T(8,128)S(1)}, bf16[1024,256]{1,0:T(8,128)(2,1)}, f32[1024]{0:T(1024)S(1)}, /*index=5*/bf16[1024,256]{1,0:T(8,128)(2,1)}, s32[]{:T(128)}) while((s32[]{:T(128)}, f32[4,512,256]{2,1,0:T(8,128)}, f32[4,512,256]{2,1,0:T(8,128)S(1)}, ...), condition=%wide.region_25.25_spmd, body=%wide.region_23.24_spmd.sunk | while | flops 538443776 | bytes 3159129 | solution.py:43
  255.0 0.2 dynamic-slice_reduce_fusion.10
  255.2 2.9 fusion.136
  258.0 0.1 dynamic-slice_reduce_fusion.10
  258.2 2.9 fusion.136
  261.0 0.1 dynamic-slice_reduce_fusion.10
  261.2 2.9 fusion.136
  264.0 0.1 dynamic-slice_reduce_fusion.10
  264.2 2.9 fusion.136
  267.1 1.6 copy.48
  268.6 2.4 scatter_custom_fusion.2
  271.1 0.0 all-reduce.23.cloned.1.call-start
  271.7 55.4 %all-reduce.17.cloned.1.call-done = f32[1024,256]{1,0:T(8,128)} async-done(((f32[1024,256]{1,0:T(8,128)}), f32[1024,256]{1,0:T(8,128)}) %all-reduce.17.cloned.1.call-update) | async-done | bytes 1048592 | tf_op jit(solution)/shard_map/psum | solution.py:67
  327.2 1.5 reduce_sum.112
  328.7 1.6 multiply_reduce_fusion.1
  330.4 1.7 fusion.58
  333.3 50.1 %all-reduce.23.cloned.1.call-done = (bf16[1024,256]{1,0:T(8,128)(2,1)}, bf16[1024,256]{1,0:T(8,128)(2,1)}) async-done(((bf16[1024,256]{1,0:T(8,128)(2,1)}, bf16[1024,256]{1,0:T(8,128)(2,1)}), (bf16[1024,256]{1,0:T(8,128)(2,1)}, bf16[1024,256]{1,0:T(8,128)(2,1)})) %all-reduce.23.cloned.1.call-update) | async-done | bytes 1048592 | tf_op jit(solution)/shard_map/psum | solution.py:9
  383.5 2.4 scatter_custom_fusion.3
  386.6 69.1 %all-reduce.19.cloned.1.call-done = f32[1024,256]{1,0:T(8,128)} async-done(((f32[1024,256]{1,0:T(8,128)}), f32[1024,256]{1,0:T(8,128)}) %all-reduce.19.cloned.1.call-update) | async-done | bytes 1048592 | tf_op jit(solution)/shard_map/psum | solution.py:67
  455.7 1.5 reduce_sum.114
  457.2 1.6 multiply_reduce_fusion
  458.8 1.7 fusion.59
  461.8 50.1 %all-reduce.21.cloned.1.call-done = (bf16[1024,256]{1,0:T(8,128)(2,1)}, bf16[1024,256]{1,0:T(8,128)(2,1)}) async-done(((bf16[1024,256]{1,0:T(8,128)(2,1)}, bf16[1024,256]{1,0:T(8,128)(2,1)}), (bf16[1024,256]{1,0:T(8,128)(2,1)}, bf16[1024,256]{1,0:T(8,128)(2,1)})) %all-reduce.21.cloned.1.call-update) | async-done | bytes 1048592 | tf_op jit(solution)/shard_map/psum | solution.py:9
  512.0 13.7 %conditional.7 = (f32[2048,256]{1,0:T(8,128)S(1)}) conditional(s32[]{:T(128)} %convert_element_type.69, f32[2048,256]{1,0:T(8,128)S(1)} %get-tuple-element.609, (f32[2048,256]{1,0:T(8,128)S(1)}, f32[4,4,1024]{2,1,0:T(4,128)S(1)}, s32[]{:T(128)}, bf16[1024,256]{1,0:T(8,128)(2,1)}, bf16[1024,256]{1,0:T(8,128)(2,1)}) %tuple.171), branch_computations={%region_43.44_spmd, %region_44.48_spmd} | conditional | flops 538443776 | bytes 7394469 | solution.py:48
  512.0 12.1 %while.45 = (s32[]{:T(128)}, f32[4,512,256]{2,1,0:T(8,128)}, f32[4,512,256]{2,1,0:T(8,128)S(1)}, bf16[1024,256]{1,0:T(8,128)(2,1)}, f32[1024]{0:T(1024)S(1)}, /*index=5*/bf16[1024,256]{1,0:T(8,128)(2,1)}, s32[]{:T(128)}) while((s32[]{:T(128)}, f32[4,512,256]{2,1,0:T(8,128)}, f32[4,512,256]{2,1,0:T(8,128)S(1)}, ...), condition=%wide.region_47.47_spmd, body=%wide.region_45.46_spmd.sunk | while | flops 538443776 | bytes 3159129 | solution.py:43
  512.0 0.2 dynamic-slice_reduce_fusion.8
  512.2 2.9 fusion.128
  515.0 0.1 dynamic-slice_reduce_fusion.8
  515.2 2.9 fusion.128
  518.0 0.1 dynamic-slice_reduce_fusion.8
  518.2 2.9 fusion.128
  521.0 0.1 dynamic-slice_reduce_fusion.8
  521.2 2.9 fusion.128
  524.1 1.6 copy.58
  525.6 1.3 copy-done
  (81 shorter events, 0.7 us)
Async XLA Ops:
  6.5 1.6 copy-start.6
  6.5 1.7 copy-start.7
  6.5 63.6 %all-reduce.13.cloned.1.call-start = ((), (), s32[]{:S(2)}) async-start(), calls=%async_computation | async-start | bytes 2097152 | tf_op jit(solution)/shard_map/psum | solution.py:67
  8.2 2.6 copy-start.10
  8.2 3.9 copy-start.8
  8.2 3.9 copy-start.9
  10.7 115.8 %all-reduce.27.cloned.1.call-start = ((), (), s32[]{:S(2)}) async-start(), calls=%async_computation.7 | async-start | bytes 2097152 | tf_op jit(solution)/shard_map/psum | solution.py:9
  70.1 3.2 copy-start.1
  71.7 4.0 copy-start.11
  71.7 54.8 %copy-start.5 = (f32[4,4,1024]{2,1,0:T(4,128)S(1)}, f32[4,4,1024]{2,1,0:T(4,128)}, u32[]{:S(2)}) copy-start(f32[4,4,1024]{2,1,0:T(4,128)} %param.31) | copy-start | bytes 196612
  75.1 123.6 %all-reduce.15.cloned.1.call-start = ((), (), s32[]{:S(2)}) async-start(), calls=%async_computation.1 | async-start | bytes 2097152 | tf_op jit(solution)/shard_map/psum | solution.py:67
  142.6 112.4 %all-reduce.25.cloned.1.call-start = ((), (), s32[]{:S(2)}) async-start(), calls=%async_computation.6 | async-start | bytes 2097152 | tf_op jit(solution)/shard_map/psum | solution.py:9
  198.7 3.2 copy-start.3
  203.6 123.6 %all-reduce.17.cloned.1.call-start = ((), (), s32[]{:S(2)}) async-start(), calls=%async_computation.2 | async-start | bytes 2097152 | tf_op jit(solution)/shard_map/psum | solution.py:67
  271.1 112.4 %all-reduce.23.cloned.1.call-start = ((), (), s32[]{:S(2)}) async-start(), calls=%async_computation.5 | async-start | bytes 2097152 | tf_op jit(solution)/shard_map/psum | solution.py:9
  327.2 3.2 copy-start.4
  332.1 123.6 %all-reduce.19.cloned.1.call-start = ((), (), s32[]{:S(2)}) async-start(), calls=%async_computation.3 | async-start | bytes 2097152 | tf_op jit(solution)/shard_map/psum | solution.py:67
  385.9 126.1 %all-reduce.21.cloned.1.call-start = ((), (), s32[]{:S(2)}) async-start(), calls=%async_computation.4 | async-start | bytes 2097152 | tf_op jit(solution)/shard_map/psum | solution.py:9
  455.7 3.2 copy-start.2
  525.6 1.3 copy-start
Sparse Core Ops, SparseCore 0:
  10.8 59.2 all-reduce.12
  75.2 51.2 all-reduce.26
  142.7 55.9 all-reduce.14
  203.7 51.2 all-reduce.24
  271.2 55.9 all-reduce.16
  332.2 51.2 all-reduce.22
  386.9 68.6 all-reduce.18
  460.7 51.2 all-reduce.20
where the time goes:
time: 534 us
  waiting for transfers between devices  438 us (82%)
  matrix products  34.3 us (6%)
  other arithmetic  21.9 us (4%)
  between operations  21.4 us (4%)
  local copies, waits for them, and re-layouts  18.1 us (3%)
    psum x4, waiting for transfers between devices, local(): prior_ens = lax.psum(padded, 'rows')  238 us
    psum x4, waiting for transfers between devices, broadcast(): return lax.psum(kept, axis)  200 us
    dot_general x12, matrix products, update_block(): jnp.dot(coupling, obs_incr, preferred_element_type=jnp.float32)  34.3 us
  transfers between devices with their start and end apart: 8, of which 8 were waited for; matrix products, arithmetic and copies ran while one was open for 0% of the time, Pallas kernels for 0%

commit v1 on v0

v1 whole, which is shorter than its diff:
```python
import functools

import jax
import jax.numpy as jnp
from jax import lax
from jax.experimental import pallas as pl
from jax.experimental.pallas import tpu as pltpu
from jax.sharding import PartitionSpec as P

MESH = pl.DeviceIdType.MESH
F32 = jnp.float32
BF16 = jnp.bfloat16
TAIL = 16
CHUNK = 128
BLOCK = 1024


def split3(value):
    high = value.astype(BF16).astype(F32)
    rest = value - high
    middle = rest.astype(BF16).astype(F32)
    return high, middle, rest - middle


def eye_mask(size):
    down = lax.broadcasted_iota(jnp.int32, (size, size), 0)
    across = lax.broadcasted_iota(jnp.int32, (size, size), 1)
    return down == across


def to_row(column, size):
    spread = jnp.broadcast_to(column, (size, size))
    return jnp.sum(jnp.where(eye_mask(size), spread, 0.0), axis=0, keepdims=True)


def to_column(row, size):
    spread = jnp.broadcast_to(row, (size, size))
    return jnp.sum(jnp.where(eye_mask(size), spread, 0.0), axis=1, keepdims=True)


def kernel(
    regions,
    group,
    owner_ref,
    readers_ref,
    obs_rows_ref,
    x_ref,
    values_ref,
    errors_ref,
    order_ref,
    taper_ref,
    out_ref,
    picked,
    z_out,
    z_in,
    full,
    prior,
    table,
    params,
    anom,
    push,
    z_send,
    z_recv,
    chip_send,
    chip_recv,
    core_send,
    core_recv,
):
    batches, obs = order_ref.shape
    rows, members = x_ref.shape
    slots = obs // group
    chips = group // 2
    steps = regions.bit_length() - 1
    block = min(BLOCK, rows, obs)
    region = lax.axis_index("region")
    me = lax.axis_index("rows")
    chip, core = me // 2, me % 2
    sibling = chip * 2 + 1 - core

    def across(step):
        bit = 2**step
        return region + bit - 2 * bit * ((region // bit) % 2)

    def z_copy(step, b):
        return pltpu.make_async_remote_copy(
            src_ref=z_out.at[step, b],
            dst_ref=z_in.at[step, b],
            send_sem=z_send.at[step, b],
            recv_sem=z_recv.at[step, b],
            device_id=(across(step), me),
            device_id_type=MESH,
        )

    def chip_copy(b, k):
        return pltpu.make_async_remote_copy(
            src_ref=full.at[b, me],
            dst_ref=full.at[b, me],
            send_sem=chip_send.at[b, k],
            recv_sem=chip_recv.at[b, k],
            device_id=(region, ((chip + k) % chips) * 2 + core),
            device_id_type=MESH,
        )

    def core_copy(b, k):
        place = ((chip + chips - k) % chips) * 2 + core
        return pltpu.make_async_remote_copy(
            src_ref=full.at[b, place],
            dst_ref=full.at[b, place],
            send_sem=core_send.at[b, k],
            recv_sem=core_recv.at[b, k],
            device_id=(region, sibling),
            device_id_type=MESH,
        )

    barrier = pltpu.get_barrier_semaphore()
    for step in range(steps):
        pl.semaphore_signal(barrier, inc=1, device_id=(across(step), me), device_id_type=MESH)
    for k in range(1, chips):
        pl.semaphore_signal(
            barrier, inc=1, device_id=(region, ((chip + k) % chips) * 2 + core), device_id_type=MESH
        )
    pl.semaphore_signal(barrier, inc=1, device_id=(region, sibling), device_id_type=MESH)

    def pick(b):
        def eight(i, carry):
            base = pl.multiple_of(i * 8, 8)
            for r in range(8):
                index = obs_rows_ref[b, me * slots + base + r]
                picked[pl.ds(base + r, 1), :] = x_ref[pl.ds(index, 1), :]
            return carry

        lax.fori_loop(0, slots // 8, eight, 0, unroll=2)
        mine = jnp.where(owner_ref[b] == region, 1.0, 0.0).astype(F32)
        held = picked[...]
        mean = jnp.mean(held, axis=1, keepdims=True)
        z_out[0, b, pl.ds(0, slots), :] = ((held - mean) * mine).astype(BF16)
        parts = split3(to_row(mean * mine, slots))
        index = lax.broadcasted_iota(jnp.int32, (TAIL, slots), 0)
        tail = jnp.zeros((TAIL, slots), F32)
        for n, part in enumerate(parts):
            tail = jnp.where(index == n, jnp.broadcast_to(part, (TAIL, slots)), tail)
        z_out[0, b, pl.ds(slots, TAIL), :] = jnp.concatenate(
            [tail, jnp.zeros((TAIL, members - slots), F32)], axis=1
        ).astype(BF16)

    def reads(b, target):
        found = owner_ref[b] == target
        for n in range(readers_ref.shape[1]):
            found = jnp.logical_or(found, readers_ref[b, n] == target)
        return jnp.where(found, 1.0, 0.0).astype(F32)

    def permute(b):
        table[0:1, :] = values_ref[b : b + 1, :]
        table[1:2, :] = errors_ref[b : b + 1, :]
        for v in range(batches):
            if v == 0:
                target = region
            elif v > b:
                target = owner_ref[v]
            else:
                continue
            table[2 + v : 3 + v, :] = taper_ref[b, pl.ds(target, 1), :] * reads(b, target)
        high, middle, low = split3(table[...])
        stacked = jnp.concatenate([high, middle, low, jnp.zeros_like(low)], axis=0).astype(BF16)
        lane = lax.broadcasted_iota(jnp.int32, (CHUNK, obs), 1).astype(F32)
        for n in range(obs // CHUNK):
            number = to_column(
                order_ref[b : b + 1, n * CHUNK : (n + 1) * CHUNK].astype(F32), CHUNK
            )
            chosen = jnp.where(number == lane, 1.0, 0.0).astype(BF16)
            got = lax.dot_general(
                chosen, stacked, (((1,), (1,)), ((), ())), preferred_element_type=F32
            )
            params[b, n * CHUNK : (n + 1) * CHUNK, :] = (
                got[:, 0:8] + got[:, 8:16] + got[:, 16:24]
            )

    def spread_out(b):
        last = steps - 1
        z_copy(last, b).wait_recv()
        full[b, me] = z_out[last, b] + z_in[last, b]
        for k in range(1, chips):
            chip_copy(b, k).start()
        core_copy(b, 0).start()

    def hand_over(b):
        for k in range(1, chips):
            chip_copy(b, k).wait_recv()
            core_copy(b, k).start()

    def place(b):
        for k in range(chips):
            core_copy(b, k).wait_recv()

        def one(g, carry):
            tail = full[b, g, pl.ds(slots, TAIL), :][:, :slots].astype(F32)
            mean = to_column(tail[0:1] + tail[1:2] + tail[2:3], slots)
            start = pl.multiple_of(b * obs + g * slots, slots)
            prior[pl.ds(start, slots), :] = full[b, g, pl.ds(0, slots), :].astype(F32) + mean
            return carry

        lax.fori_loop(0, group, one, 0, unroll=4)

    def prepare(b):
        def one(n, carry):
            start = pl.multiple_of(n * CHUNK, CHUNK)
            held = prior[pl.ds(b * obs + start, CHUNK), :]
            param = params[b, pl.ds(start, CHUNK), :]
            value, error = param[:, 0:1], param[:, 1:2]
            mean = jnp.mean(held, axis=1, keepdims=True)
            away = held - mean
            variance = jnp.sum(away * away, axis=1, keepdims=True) / (members - 1) + 1e-05
            total = 1.0 / (variance + error)
            shift = variance * (value - mean) * total
            shrink = jnp.sqrt(error * total)
            increment = shift + (shrink - 1.0) * away
            anom[pl.ds(start, CHUNK), :] = away.astype(BF16)
            inverse = 1.0 / ((members - 1) * variance)
            for v in range(batches):
                if v == 0 or v > b:
                    weight = param[:, 2 + v : 3 + v] * inverse
                    push[v, pl.ds(start, CHUNK), :] = (increment * weight).astype(BF16)
            return carry

        lax.fori_loop(0, obs // CHUNK, one, 0, unroll=4)

    def updated(held, variant):
        mean = jnp.mean(held, axis=1, keepdims=True)
        away = (held - mean).astype(BF16)
        linked = lax.dot_general(
            away, anom[...], (((1,), (1,)), ((), ())), preferred_element_type=F32
        ).astype(BF16)
        return held + jnp.dot(linked, push[variant], preferred_element_type=F32)

    def observed(b, first, last):
        per = obs // block

        def one(i, carry):
            at = pl.ds(pl.multiple_of(i * block, block), block)
            prior[at, :] = updated(prior[at, :], i // per)
            return carry

        lax.fori_loop(first * per, last * per, one, 0)

    def state(b, source, first, last):
        def one(i, carry):
            at = pl.ds(pl.multiple_of(i * wide, wide), wide)
            out_ref[at, :] = updated(source[at, :], 0)
            return carry

        lax.fori_loop(first, last, one, 0)

    pick(0)
    pl.semaphore_wait(barrier, steps + chips)
    z_copy(0, 0).start()
    for b in range(1, batches):
        pick(b)
        z_copy(0, b).start()
    table[...] = jnp.zeros_like(table)
    permute(0)
    for step in range(1, steps):
        for b in range(batches):
            z_copy(step - 1, b).wait_recv()
            z_out[step, b] = z_out[step - 1, b] + z_in[step - 1, b]
            z_copy(step, b).start()
    wide = min(2 * BLOCK, rows)
    blocks = rows // wide
    for b in range(1, batches):
        spread_out(b - 1)
        if b > 1:
            hand_over(b - 2)
        permute(b)
        if b == 2:
            place(0)
            prepare(0)
    spread_out(batches - 1)
    pending = [batches - 2, batches - 1]
    hand_over(pending[0])
    state(0, x_ref, 0, blocks)
    hand_over(pending[1])
    for b in range(1, batches):
        place(b)
        observed(0, b, b + 1)
    for b in range(1, batches):
        prepare(b)
        if b + 1 < batches:
            observed(b, b + 1, batches)
        state(b, out_ref, 0, blocks)
    for b in range(batches):
        for step in range(steps):
            z_copy(step, b).wait_send()
        for k in range(chips):
            if k:
                chip_copy(b, k).wait_send()
            core_copy(b, k).wait_send()


def local(regions, group, state, values, errors, owner, readers, order, obs_rows, taper):
    batches, obs = order.shape
    rows, members = state.shape
    slots = obs // group
    chips = group // 2
    steps = regions.bit_length() - 1
    packet = (slots + TAIL, members)
    smem = pl.BlockSpec(memory_space=pltpu.SMEM)
    vmem = pl.BlockSpec(memory_space=pltpu.VMEM)
    dma = pltpu.SemaphoreType.DMA
    return pl.pallas_call(
        functools.partial(kernel, regions, group),
        out_shape=jax.ShapeDtypeStruct((rows, members), F32),
        in_specs=[smem] * 3 + [vmem] * 5,
        out_specs=vmem,
        scratch_shapes=[
            pltpu.VMEM((slots, members), F32),
            pltpu.VMEM((steps, batches) + packet, BF16),
            pltpu.VMEM((steps, batches) + packet, BF16),
            pltpu.VMEM((batches, group) + packet, BF16),
            pltpu.VMEM((batches * obs, members), F32),
            pltpu.VMEM((8, obs), F32),
            pltpu.VMEM((batches, obs, 8), F32),
            pltpu.VMEM((obs, members), BF16),
            pltpu.VMEM((batches, obs, members), BF16),
            dma((steps, batches)),
            dma((steps, batches)),
            dma((batches, chips)),
            dma((batches, chips)),
            dma((batches, chips)),
            dma((batches, chips)),
        ],
        compiler_params=pltpu.CompilerParams(
            collective_id=0, has_side_effects=True, vmem_limit_bytes=63 * 2**20
        ),
    )(owner, readers, obs_rows, state, values, errors, order, taper)


def solution(mesh):
    placed = (P(("region", "rows"), None), P(), P(), P(), P(), P(), P(), P())
    return jax.shard_map(
        functools.partial(local, mesh.shape["region"], mesh.shape["rows"]),
        mesh=mesh,
        in_specs=placed,
        out_specs=P(("region", "rows"), None),
        check_vma=False,
    )
```

time: 534 us -> 67.6 us (0.13)
  waiting for transfers between devices: 438 us -> 0 us
  Pallas kernels: 0 us -> 64.4 us
  matrix products: 34.3 us -> 0 us
  other arithmetic: 21.9 us -> 0 us
  between operations: 21.4 us -> 0.01 us
  local copies, waits for them, and re-layouts: 18.1 us -> 3.05 us
    psum x8 -> x0, waiting for transfers between devices: 438 us -> none  [the longest x4 238 us: local(): prior_ens = lax.psum(padded, 'rows')]
    pallas_call x0 -> x1, Pallas kernels: none -> 64.4 us  [local(): pl.pallas_call(functools.partial(kernel, regions, group), out_shape=jax.S...]
    dot_general x12 -> x0, matrix products: 34.3 us -> none  [update_block(): jnp.dot(coupling, obs_incr, preferred_element_type=jnp.float32)]
    reduce_sum x20 -> x0, other arithmetic: 14.2 us -> none  [the longest x4 6.37 us: adjust(): jnp.sum(anomalies * anomalies, axis=1, keepdims=True) / (members - 1)]
    scatter x4 -> x0, local copies, waits for them, and re-layouts: 9.55 us -> none  [local(): padded = jnp.zeros((obs_count, members), jnp.float32).at[placed].set(pieces)]
    select_n x11 -> x0, other arithmetic: 6.82 us -> none  [the longest x4 6.74 us: broadcast(): jnp.where(lax.axis_index(axis) == source, value, 0).astype(value.dtype)]
  transfers between devices with their start and end apart: 8 -> 0, of which waited for: 8 -> 0; matrix products, arithmetic and copies ran while one was open for 0% -> 0% of each run, Pallas kernels for 0% -> 0%
where the time goes in v1:
time: 67.6 us; the launch traced here: 67.4 us
  Pallas kernels  64.4 us (95%)
  local copies, waits for them, and re-layouts  3.05 us (5%)
    pallas_call x1, Pallas kernels, local(): pl.pallas_call(functools.partial(kernel, regions, group), out_shape=jax.S...  64.4 us
    unnamed x1, local copies, waits for them, and re-layouts  3.05 us

profile of v1, /device:TPU:0, one launch (start us, length us, event | category | flops | bytes accessed | tf_op | source)
XLA Modules:
  0.0 67.4 jit_solution(11886611376848836851)
XLA Ops:
  0.0 64.4 %shard_map.82 = f32[2048,256]{1,0:T(8,128)} custom-call(s32[4]{0:T(128)} %owner_ref.1, s32[4,3]{1,0:T(4,128)} %readers_ref.1, s32[4,1024]{1,0:T(4,128)} %obs_rows_ref.1, f32[2048,256]{1,0:T(8,128)} %x_ref.1, f32[4,1024]{1,0:T(4,128)} %values_ref.1, f32[4,1024]{1,0:T(4,128)} %errors_ref.1, s32[4,1024]{1,0:T(4,128)} %order_ref.1, f32[4,4,1024]{2,1,0:T(4,128)} %taper_ref.1), custom_call_target="tpu_custom_call" | custom-call | tf_op jit(solution)/shard_map/pallas_call | solution.py:308
  64.4 3.0 %copy.10 = f32[2048,256]{1,0:T(8,128)} copy(f32[2048,256]{1,0:T(8,128)} %shard_map.82) | data formatting | bytes 4194304

commit v2 on v1

--- a/solution.py
+++ b/solution.py
@@ -65,13 +65,15 @@
     chip_recv,
     core_send,
     core_recv,
+    half_send,
+    half_recv,
 ):
     batches, obs = order_ref.shape
     rows, members = x_ref.shape
     slots = obs // group
     chips = group // 2
     steps = regions.bit_length() - 1
-    block = min(BLOCK, rows, obs)
+    half = obs // 2
     region = lax.axis_index("region")
     me = lax.axis_index("rows")
     chip, core = me // 2, me % 2
@@ -108,6 +110,17 @@
             dst_ref=full.at[b, place],
             send_sem=core_send.at[b, k],
             recv_sem=core_recv.at[b, k],
+            device_id=(region, sibling),
+            device_id_type=MESH,
+        )
+
+    def half_copy(b):
+        part = prior.at[pl.ds(pl.multiple_of(b * obs + core * half, half), half)]
+        return pltpu.make_async_remote_copy(
+            src_ref=part,
+            dst_ref=part,
+            send_sem=half_send.at[b],
+            recv_sem=half_recv.at[b],
             device_id=(region, sibling),
             device_id_type=MESH,
         )
@@ -199,7 +212,12 @@
             prior[pl.ds(start, slots), :] = full[b, g, pl.ds(0, slots), :].astype(F32) + mean
             return carry
 
-        lax.fori_loop(0, group, one, 0, unroll=4)
+        if b == 0:
+            lax.fori_loop(0, group, one, 0, unroll=4)
+        else:
+            lax.fori_loop(
+                0, chips, lambda n, carry: one(core * chips + n, carry), 0, unroll=4
+            )
 
     def prepare(b):
         def one(n, carry):
@@ -233,14 +251,11 @@
         return held + jnp.dot(linked, push[variant], preferred_element_type=F32)
 
     def observed(b, first, last):
-        per = obs // block
-
-        def one(i, carry):
-            at = pl.ds(pl.multiple_of(i * block, block), block)
-            prior[at, :] = updated(prior[at, :], i // per)
-            return carry
-
-        lax.fori_loop(first * per, last * per, one, 0)
+        for c in range(first, last):
+            at = pl.ds(pl.multiple_of(c * obs + core * half, half), half)
+            prior[at, :] = updated(prior[at, :], c)
+            if c == b + 1:
+                half_copy(c).start()
 
     def state(b, source, first, last):
         def one(i, carry):
@@ -282,9 +297,9 @@
         place(b)
         observed(0, b, b + 1)
     for b in range(1, batches):
+        half_copy(b).wait_recv()
         prepare(b)
-        if b + 1 < batches:
-            observed(b, b + 1, batches)
+        observed(b, b + 1, batches)
         state(b, out_ref, 0, blocks)
     for b in range(batches):
         for step in range(steps):
@@ -293,6 +308,8 @@
             if k:
                 chip_copy(b, k).wait_send()
             core_copy(b, k).wait_send()
+        if b:
+            half_copy(b).wait_send()
 
 
 def local(regions, group, state, values, errors, owner, readers, order, obs_rows, taper):
@@ -326,6 +343,8 @@
             dma((batches, chips)),
             dma((batches, chips)),
             dma((batches, chips)),
+            dma((batches,)),
+            dma((batches,)),
         ],
         compiler_params=pltpu.CompilerParams(
             collective_id=0, has_side_effects=True, vmem_limit_bytes=63 * 2**20

time: 67.6 us -> 66.3 us (0.981)
  Pallas kernels: 64.4 us -> 63.1 us
    pallas_call x1, Pallas kernels: 64.4 us -> 63.1 us  [local(): pl.pallas_call(functools.partial(kernel, regions, group), out_shape=jax.S...]
where the time goes in v2:
time: 66.3 us; the launch traced here: 66.2 us
  Pallas kernels  63.1 us (95%)
  local copies, waits for them, and re-layouts  3.05 us (5%)
    pallas_call x1, Pallas kernels, local(): pl.pallas_call(functools.partial(kernel, regions, group), out_shape=jax.S...  63.1 us
    unnamed x1, local copies, waits for them, and re-layouts  3.05 us

profile of v2, /device:TPU:0, one launch (start us, length us, event | category | flops | bytes accessed | tf_op | source)
XLA Modules:
  0.0 66.2 jit_solution(553429488867736291)
XLA Ops:
  0.0 63.1 %shard_map.82 = f32[2048,256]{1,0:T(8,128)} custom-call(s32[4]{0:T(128)} %owner_ref.1, s32[4,3]{1,0:T(4,128)} %readers_ref.1, s32[4,1024]{1,0:T(4,128)} %obs_rows_ref.1, f32[2048,256]{1,0:T(8,128)} %x_ref.1, f32[4,1024]{1,0:T(4,128)} %values_ref.1, f32[4,1024]{1,0:T(4,128)} %errors_ref.1, s32[4,1024]{1,0:T(4,128)} %order_ref.1, f32[4,4,1024]{2,1,0:T(4,128)} %taper_ref.1), custom_call_target="tpu_custom_call" | custom-call | tf_op jit(solution)/shard_map/pallas_call | solution.py:325
  63.1 3.0 %copy.10 = f32[2048,256]{1,0:T(8,128)} copy(f32[2048,256]{1,0:T(8,128)} %shard_map.82) | data formatting | bytes 4194304
